TPU v7x, 32 devices: a whole 2x2x4 slice. The times are simulated.
32 devices in a mesh: row: 16 (over z, y, x), col: 2 (over core).
Axes of the slice: x: 2, y: 2, z: 4, core: 2. Of those that a mesh axis runs over, the one named last changes fastest.
Arguments:
- right_side: float32 [12288, 1280], P('row', 'col'), may hold values from -6 to 6
- factor_panel: bfloat16 [512, 3, 12288], P('col', None, 'row'), may hold values from -0.15625 to 0.15625
- diag_inverse: float32 [3, 512, 512], P(None, 'row'), may hold values from -1.5 to 1.5, as said below
Outputs:
- solved: float32 [12288, 1280], P('row', 'col')
Inputs may be any that keep to these rules, and one draw needn't show every extreme that they name: `diag_inverse`: each of the 3 blocks is zero above its diagonal; its diagonal lies between 0.5 and 1.5.
All inputs are finite; a program needn't handle non-finite values.
Results may differ from a plain program's by a relative error of at most 0.003.
Values may be sent and summed in bfloat16 or wider, within the bound.
A program may use at most 64 MiB of HBM per device.

v0:
```python
import jax
import jax.numpy as jnp
from jax import lax
from jax.sharding import PartitionSpec as P

KB = 3


def shards(right_side, factor_panel, diag_inverse):
    local_rows = right_side.shape[0]
    block_rows = diag_inverse.shape[1]
    workspace = right_side
    for step_index in reversed(range(KB)):
        offset = local_rows - (KB - step_index) * block_rows
        block_rhs = workspace[offset : offset + block_rows]
        partial_value = lax.dot_general(
            diag_inverse[step_index],
            block_rhs,
            (((0,), (0,)), ((), ())),
            precision=lax.Precision.HIGHEST,
            preferred_element_type=jnp.float32,
        )
        whole_x = lax.psum(partial_value, "row")
        own_rows = lax.dynamic_slice_in_dim(
            whole_x, lax.axis_index("row") * block_rows, block_rows, 0
        )
        block_low = whole_x.astype(jnp.bfloat16)
        update = lax.dot_general(
            lax.all_gather(factor_panel[:, step_index, :offset], "col", axis=0, tiled=True),
            block_low,
            (((0,), (0,)), ((), ())),
            preferred_element_type=jnp.float32,
        )
        workspace = jnp.concatenate(
            [workspace[:offset] - update, own_rows, workspace[offset + block_rows :]], axis=0
        )
    return workspace


def solution(mesh):
    placed = (P("row", "col"), P("col", None, "row"), P(None, "row", None))
    return jax.shard_map(
        shards, mesh=mesh, in_specs=placed, out_specs=P("row", "col"), check_vma=False
    )
```

profile of v0, /device:TPU:0, one launch (start us, length us, event | category | flops | bytes accessed | tf_op | source)
XLA Modules:
  0.0 380.1 jit_solution(885599477888310501)
XLA Ops:
  6.5 0.0 all-reduce.4.cloned.1.call-start
  6.5 3.2 fusion.8
  9.8 0.0 all-reduce.4.cloned.1.call-update
  9.8 0.0 all-reduce.6.cloned.1.call-start
  9.8 1.0 slice.39
  10.9 2.4 all-gather
  13.3 0.0 copy-start.2
  13.3 117.0 %all-reduce.4.cloned.1.call-done = f32[512,640]{1,0:T(8,128)} async-done(((f32[512,640]{1,0:T(8,128)}), f32[512,640]{1,0:T(8,128)}) %all-reduce.4.cloned.1.call-update) | async-done | bytes 1310736 | tf_op jit(solution)/shard_map/psum | solution.py:23
  130.3 2.7 bitcast_subtract_fusion
  133.0 0.0 copy-done.2
  133.0 2.3 convolution_bitcast_fusion.1
  135.3 0.0 all-reduce.6.cloned.1.call-update
  135.3 0.0 all-reduce.8.cloned.1.call-start
  135.4 1.0 slice.43
  136.4 2.4 all-gather.1
  138.7 111.2 %all-reduce.6.cloned.1.call-done = f32[512,640]{1,0:T(8,128)} async-done(((f32[512,640]{1,0:T(8,128)}), f32[512,640]{1,0:T(8,128)}) %all-reduce.6.cloned.1.call-update) | async-done | bytes 1310736 | tf_op jit(solution)/shard_map/psum | solution.py:23
  249.9 2.1 slice_subtract_fusion
  252.1 0.0 copy-start
  252.1 1.2 copy-done
  253.3 2.3 convolution_bitcast_fusion
  255.6 0.0 copy-start.1
  255.6 0.0 all-reduce.8.cloned.1.call-update
  255.6 1.2 slice.47
  256.8 2.4 all-gather.2
  259.1 0.9 constant_dynamic-slice_fusion
  260.1 0.9 constant_dynamic-slice_fusion.1
  261.0 108.2 %all-reduce.8.cloned.1.call-done = f32[512,640]{1,0:T(8,128)} async-done(((f32[512,640]{1,0:T(8,128)}), f32[512,640]{1,0:T(8,128)}) %all-reduce.8.cloned.1.call-update) | async-done | bytes 1310736 | tf_op jit(solution)/shard_map/psum | solution.py:23
  369.2 0.9 constant_dynamic-slice_fusion.2
  370.1 0.0 copy-done.1
  370.1 2.1 slice_subtract_fusion.1
  372.2 1.4 pad_maximum_fusion
Async XLA Ops:
  6.5 123.7 %all-reduce.4.cloned.1.call-start = ((), (), s32[]{:S(2)}) async-start(), calls=%async_computation | async-start | bytes 2621440 | tf_op jit(solution)/shard_map/psum | solution.py:23
  9.8 240.2 %all-reduce.6.cloned.1.call-start = ((), (), s32[]{:S(2)}) async-start(), calls=%async_computation.1 | async-start | bytes 2621440 | tf_op jit(solution)/shard_map/psum | solution.py:23
  13.3 119.7 %copy-start.2 = (f32[3,32,512]{2,1,0:T(8,128)S(1)}, f32[3,32,512]{2,1,0:T(8,128)}, u32[]{:S(2)}) copy-start(f32[3,32,512]{2,1,0:T(8,128)} %param.5) | copy-start | bytes 589828
  135.3 233.9 %all-reduce.8.cloned.1.call-start = ((), (), s32[]{:S(2)}) async-start(), calls=%async_computation.2 | async-start | bytes 2621440 | tf_op jit(solution)/shard_map/psum | solution.py:23
  252.1 1.2 copy-start
  255.6 114.5 %copy-start.1 = (f32[704,640]{1,0:T(8,128)S(1)}, f32[704,640]{1,0:T(8,128)}, u32[]{:S(2)}) copy-start(f32[704,640]{1,0:T(8,128)} %copy-done) | copy-start | bytes 5406724
Sparse Core Ops, SparseCore 0:
  12.8 117.4 all-reduce.3
  136.5 113.3 all-reduce.5
  255.7 113.4 all-reduce.7
where the time goes:
time: 381 us; the launch traced here: 380 us
  waiting for transfers between devices  336 us (88%)
  matrix products  14.7 us (4%)
  between operations  13.2 us (3%)
  blocking collectives  7.18 us (2%)
  local copies, waits for them, and re-layouts  7.14 us (2%)
    psum x3, waiting for transfers between devices, shards(): whole_x = lax.psum(partial_value, 'row')  336 us
    dot_general x3, matrix products, shards(): lax.dot_general(diag_inverse[step_index], block_rhs, (((0,), (0,)), ((),...  7.79 us
  transfers between devices with their start and end apart: 3, of which 3 were waited for; matrix products, arithmetic and copies ran while one was open for 1% of the time, Pallas kernels for 0%

commit v1 on v0

--- a/solution.py
+++ b/solution.py
@@ -20,7 +20,11 @@
             precision=lax.Precision.HIGHEST,
             preferred_element_type=jnp.float32,
         )
-        whole_x = lax.psum(partial_value, "row")
+        whole_x = partial_value
+        for hop in (1, 2, 4, 8):
+            whole_x = whole_x + lax.ppermute(
+                whole_x, "row", [(dev, dev ^ hop) for dev in range(16)]
+            )
         own_rows = lax.dynamic_slice_in_dim(
             whole_x, lax.axis_index("row") * block_rows, block_rows, 0
         )

time: 381 us -> 455 us (1.19)
  waiting for transfers between devices: 336 us -> 409 us
  starting transfers between devices: 0.09 us -> 23.7 us
  between operations: 13.2 us -> 0.15 us
  matrix products: 14.7 us -> 7.02 us
  local copies, waits for them, and re-layouts: 7.14 us -> 1.32 us
    ppermute x0 -> x12, waiting for transfers between devices: none -> 409 us  [shards(): lax.ppermute(whole_x, 'row', [(dev, dev ^ hop) for dev in range(16)])]
    psum x3 -> x0, waiting for transfers between devices: 336 us -> none  [shards(): whole_x = lax.psum(partial_value, 'row')]
    ppermute x0 -> x12, starting transfers between devices: none -> 23.7 us  [shards(): lax.ppermute(whole_x, 'row', [(dev, dev ^ hop) for dev in range(16)])]
  transfers between devices with their start and end apart: 3 -> 12, of which waited for: 3 -> 12; matrix products, arithmetic and copies ran while one was open for 1% -> 0% of each run, Pallas kernels for 0% -> 0%
where the time goes in v1:
time: 455 us; the launch traced here: 454 us
  waiting for transfers between devices  409 us (90%)
  starting transfers between devices  23.7 us (5%)
  blocking collectives  7.11 us (2%)
  matrix products  7.02 us (2%)
  other arithmetic  5.78 us (1%)
    ppermute x12, waiting for transfers between devices, shards(): lax.ppermute(whole_x, 'row', [(dev, dev ^ hop) for dev in range(16)])  409 us
    ppermute x12, starting transfers between devices, shards(): lax.ppermute(whole_x, 'row', [(dev, dev ^ hop) for dev in range(16)])  23.7 us
  transfers between devices with their start and end apart: 12, of which 12 were waited for; matrix products, arithmetic and copies ran while one was open for 0% of the time, Pallas kernels for 0%

profile of v1, /device:TPU:0, one launch (start us, length us, event | category | flops | bytes accessed | tf_op | source)
XLA Modules:
  0.0 454.2 jit_solution(6582658932754789972)
XLA Ops:
  0.0 2.2 fusion.8
  2.2 3.0 collective-permute-start
  5.2 28.8 %collective-permute-done = f32[512,640]{1,0:T(8,128)S(1)} collective-permute-done((f32[512,640]{1,0:T(8,128)S(1)}, f32[512,640]{1,0:T(8,128)S(1)}, u32[]{:S(2)}, u32[]{:S(2)}) %collective-permute-start) | collective-permute-done | bytes 1310752 | tf_op jit(solution)/shard_map/ppermute | solution.py:25
  34.0 0.1 add.41
  34.1 1.8 collective-permute-start.1
  35.9 28.2 %collective-permute-done.1 = f32[512,640]{1,0:T(8,128)S(1)} collective-permute-done((f32[512,640]{1,0:T(8,128)S(1)}, f32[512,640]{1,0:T(8,128)S(1)}, u32[]{:S(2)}, u32[]{:S(2)}) %collective-permute-start.1) | collective-permute-done | bytes 1310752 | tf_op jit(solution)/shard_map/ppermute | solution.py:25
  64.1 0.1 add.42
  64.3 1.6 collective-permute-start.2
  65.8 27.5 %collective-permute-done.2 = f32[512,640]{1,0:T(8,128)S(1)} collective-permute-done((f32[512,640]{1,0:T(8,128)S(1)}, f32[512,640]{1,0:T(8,128)S(1)}, u32[]{:S(2)}, u32[]{:S(2)}) %collective-permute-start.2) | collective-permute-done | bytes 1310752 | tf_op jit(solution)/shard_map/ppermute | solution.py:25
  93.4 0.1 add.43
  93.5 2.4 collective-permute-start.3
  95.9 2.4 all-gather
  98.3 52.4 %collective-permute-done.3 = f32[512,640]{1,0:T(8,128)S(1)} collective-permute-done((f32[512,640]{1,0:T(8,128)S(1)}, f32[512,640]{1,0:T(8,128)S(1)}, u32[]{:S(2)}, u32[]{:S(2)}) %collective-permute-start.3) | collective-permute-done | bytes 1310752 | tf_op jit(solution)/shard_map/ppermute | solution.py:25
  150.7 0.1 add.44
  150.8 0.8 bitcast_subtract_fusion
  151.8 1.2 convolution_bitcast_fusion.1
  153.0 0.9 collective-permute-start.4
  153.9 29.4 %collective-permute-done.4 = f32[512,640]{1,0:T(8,128)S(1)} collective-permute-done((f32[512,640]{1,0:T(8,128)S(1)}, f32[512,640]{1,0:T(8,128)S(1)}, u32[]{:S(2)}, u32[]{:S(2)}) %collective-permute-start.4) | collective-permute-done | bytes 1310752 | tf_op jit(solution)/shard_map/ppermute | solution.py:25
  183.2 0.1 add.45
  183.3 0.1 collective-permute-start.5
  183.5 29.2 %collective-permute-done.5 = f32[512,640]{1,0:T(8,128)S(1)} collective-permute-done((f32[512,640]{1,0:T(8,128)S(1)}, f32[512,640]{1,0:T(8,128)S(1)}, u32[]{:S(2)}, u32[]{:S(2)}) %collective-permute-start.5) | collective-permute-done | bytes 1310752 | tf_op jit(solution)/shard_map/ppermute | solution.py:25
  212.6 0.1 add.46
  212.8 1.2 collective-permute-start.6
  213.9 27.2 %collective-permute-done.6 = f32[512,640]{1,0:T(8,128)S(1)} collective-permute-done((f32[512,640]{1,0:T(8,128)S(1)}, f32[512,640]{1,0:T(8,128)S(1)}, u32[]{:S(2)}, u32[]{:S(2)}) %collective-permute-start.6) | collective-permute-done | bytes 1310752 | tf_op jit(solution)/shard_map/ppermute | solution.py:25
  241.1 0.1 add.47
  241.3 3.4 collective-permute-start.7
  244.7 2.4 all-gather.1
  247.1 52.2 %collective-permute-done.7 = f32[512,640]{1,0:T(8,128)S(1)} collective-permute-done((f32[512,640]{1,0:T(8,128)S(1)}, f32[512,640]{1,0:T(8,128)S(1)}, u32[]{:S(2)}, u32[]{:S(2)}) %collective-permute-start.7) | collective-permute-done | bytes 1310752 | tf_op jit(solution)/shard_map/ppermute | solution.py:25
  299.3 0.1 add.48
  299.5 0.8 slice_subtract_fusion
  300.3 0.2 copy-done
  300.5 1.2 convolution_bitcast_fusion
  301.8 1.6 collective-permute-start.8
  303.4 28.2 %collective-permute-done.8 = f32[512,640]{1,0:T(8,128)S(1)} collective-permute-done((f32[512,640]{1,0:T(8,128)S(1)}, f32[512,640]{1,0:T(8,128)S(1)}, u32[]{:S(2)}, u32[]{:S(2)}) %collective-permute-start.8) | collective-permute-done | bytes 1310752 | tf_op jit(solution)/shard_map/ppermute | solution.py:25
  331.6 0.1 add.49
  331.7 1.6 collective-permute-start.9
  333.3 27.3 %collective-permute-done.9 = f32[512,640]{1,0:T(8,128)S(1)} collective-permute-done((f32[512,640]{1,0:T(8,128)S(1)}, f32[512,640]{1,0:T(8,128)S(1)}, u32[]{:S(2)}, u32[]{:S(2)}) %collective-permute-start.9) | collective-permute-done | bytes 1310752 | tf_op jit(solution)/shard_map/ppermute | solution.py:25
  360.6 0.1 add.50
  360.7 2.8 collective-permute-start.10
  363.5 27.2 %collective-permute-done.10 = f32[512,640]{1,0:T(8,128)S(1)} collective-permute-done((f32[512,640]{1,0:T(8,128)S(1)}, f32[512,640]{1,0:T(8,128)S(1)}, u32[]{:S(2)}, u32[]{:S(2)}) %collective-permute-start.10) | collective-permute-done | bytes 1310752 | tf_op jit(solution)/shard_map/ppermute | solution.py:25
  390.7 1.2 add.51
  391.9 3.4 collective-permute-start.11
  395.3 2.4 all-gather.2
  397.7 0.9 constant_dynamic-slice_fusion.1
  398.6 51.6 %collective-permute-done.11 = f32[512,640]{1,0:T(8,128)} collective-permute-done((f32[512,640]{1,0:T(8,128)}, f32[512,640]{1,0:T(8,128)}, u32[]{:S(2)}, u32[]{:S(2)}) %collective-permute-start.11) | collective-permute-done | bytes 1310752 | tf_op jit(solution)/shard_map/ppermute | solution.py:25
  450.2 1.8 add.52
  452.1 0.8 slice_subtract_fusion.1
  452.8 1.4 pad_maximum_fusion
  (12 shorter events, 0.2 us)
Async XLA Ops:
  2.2 31.8 %collective-permute-start = (f32[512,640]{1,0:T(8,128)S(1)}, f32[512,640]{1,0:T(8,128)S(1)}, u32[]{:S(2)}, u32[]{:S(2)}) collective-permute-start(f32[512,640]{1,0:T(8,128)S(1)} %fusion.8), channel_id=1, source_target_pairs={{0,2},{2,0},{4,6},{6,4},{8,10},{10,8},{12,14},{14,12},{16,18},{18,... | collective-permute-start | bytes 3932168 | tf_op jit(solution)/shard_map/ppermute | solution.py:25
  34.1 30.0 %collective-permute-start.1 = (f32[512,640]{1,0:T(8,128)S(1)}, f32[512,640]{1,0:T(8,128)S(1)}, u32[]{:S(2)}, u32[]{:S(2)}) collective-permute-start(f32[512,640]{1,0:T(8,128)S(1)} %add.41), channel_id=1, source_target_pairs={{0,4},{2,6},{4,0},{6,2},{8,12},{10,14},{12,8},{14,10},{16,20},{18,... | collective-permute-start | bytes 3932168 | tf_op jit(solution)/shard_map/ppermute | solution.py:25
  64.3 31.6 %copy-start.2 = (bf16[256,3,768]{2,0,1:T(8,128)(2,1)S(1)}, bf16[256,3,768]{2,0,1:T(8,128)(2,1)}, u32[]{:S(2)}) copy-start(bf16[256,3,768]{2,0,1:T(8,128)(2,1)} %param.4) | copy-start | bytes 3538948
  64.3 29.1 %collective-permute-start.2 = (f32[512,640]{1,0:T(8,128)S(1)}, f32[512,640]{1,0:T(8,128)S(1)}, u32[]{:S(2)}, u32[]{:S(2)}) collective-permute-start(f32[512,640]{1,0:T(8,128)S(1)} %add.42), channel_id=1, source_target_pairs={{0,8},{2,10},{4,12},{6,14},{8,0},{10,2},{12,4},{14,6},{16,24},{18,... | collective-permute-start | bytes 3932168 | tf_op jit(solution)/shard_map/ppermute | solution.py:25
  93.5 57.2 %collective-permute-start.3 = (f32[512,640]{1,0:T(8,128)S(1)}, f32[512,640]{1,0:T(8,128)S(1)}, u32[]{:S(2)}, u32[]{:S(2)}) collective-permute-start(f32[512,640]{1,0:T(8,128)S(1)} %add.43), channel_id=1, source_target_pairs={{0,16},{2,18},{4,20},{6,22},{8,24},{10,26},{12,28},{14,30},{16,0},... | collective-permute-start | bytes 3932168 | tf_op jit(solution)/shard_map/ppermute | solution.py:25
  98.3 52.5 %copy-start.1 = (f32[768,640]{1,0:T(8,128)S(1)}, f32[768,640]{1,0:T(8,128)}, u32[]{:S(2)}) copy-start(f32[768,640]{1,0:T(8,128)} %param.3) | copy-start | bytes 5898244
  150.8 0.9 copy-start.3
  153.0 30.2 %collective-permute-start.4 = (f32[512,640]{1,0:T(8,128)S(1)}, f32[512,640]{1,0:T(8,128)S(1)}, u32[]{:S(2)}, u32[]{:S(2)}) collective-permute-start(f32[512,640]{1,0:T(8,128)S(1)} %convolution_bitcast_fusion.1), channel_id=1, source_target_pairs={{0,2},{2,0},{4,6},{6,4},{8,10},{10,8},{12,14},{14,12},{16,18},{18,... | collective-permute-start | bytes 3932168 | tf_op jit(solution)/shard_map/ppermute | solution.py:25
  183.3 29.3 %collective-permute-start.5 = (f32[512,640]{1,0:T(8,128)S(1)}, f32[512,640]{1,0:T(8,128)S(1)}, u32[]{:S(2)}, u32[]{:S(2)}) collective-permute-start(f32[512,640]{1,0:T(8,128)S(1)} %add.45), channel_id=1, source_target_pairs={{0,4},{2,6},{4,0},{6,2},{8,12},{10,14},{12,8},{14,10},{16,20},{18,... | collective-permute-start | bytes 3932168 | tf_op jit(solution)/shard_map/ppermute | solution.py:25
  212.8 28.4 %collective-permute-start.6 = (f32[512,640]{1,0:T(8,128)S(1)}, f32[512,640]{1,0:T(8,128)S(1)}, u32[]{:S(2)}, u32[]{:S(2)}) collective-permute-start(f32[512,640]{1,0:T(8,128)S(1)} %add.46), channel_id=1, source_target_pairs={{0,8},{2,10},{4,12},{6,14},{8,0},{10,2},{12,4},{14,6},{16,24},{18,... | collective-permute-start | bytes 3932168 | tf_op jit(solution)/shard_map/ppermute | solution.py:25
  241.3 58.1 %collective-permute-start.7 = (f32[512,640]{1,0:T(8,128)S(1)}, f32[512,640]{1,0:T(8,128)S(1)}, u32[]{:S(2)}, u32[]{:S(2)}) collective-permute-start(f32[512,640]{1,0:T(8,128)S(1)} %add.47), channel_id=1, source_target_pairs={{0,16},{2,18},{4,20},{6,22},{8,24},{10,26},{12,28},{14,30},{16,0},... | collective-permute-start | bytes 3932168 | tf_op jit(solution)/shard_map/ppermute | solution.py:25
  299.5 1.1 copy-start
  301.8 29.8 %collective-permute-start.8 = (f32[512,640]{1,0:T(8,128)S(1)}, f32[512,640]{1,0:T(8,128)S(1)}, u32[]{:S(2)}, u32[]{:S(2)}) collective-permute-start(f32[512,640]{1,0:T(8,128)S(1)} %convolution_bitcast_fusion), channel_id=1, source_target_pairs={{0,2},{2,0},{4,6},{6,4},{8,10},{10,8},{12,14},{14,12},{16,18},{18,... | collective-permute-start | bytes 3932168 | tf_op jit(solution)/shard_map/ppermute | solution.py:25
  331.7 28.9 %collective-permute-start.9 = (f32[512,640]{1,0:T(8,128)S(1)}, f32[512,640]{1,0:T(8,128)S(1)}, u32[]{:S(2)}, u32[]{:S(2)}) collective-permute-start(f32[512,640]{1,0:T(8,128)S(1)} %add.49), channel_id=1, source_target_pairs={{0,4},{2,6},{4,0},{6,2},{8,12},{10,14},{12,8},{14,10},{16,20},{18,... | collective-permute-start | bytes 3932168 | tf_op jit(solution)/shard_map/ppermute | solution.py:25
  360.7 30.0 %collective-permute-start.10 = (f32[512,640]{1,0:T(8,128)S(1)}, f32[512,640]{1,0:T(8,128)S(1)}, u32[]{:S(2)}, u32[]{:S(2)}) collective-permute-start(f32[512,640]{1,0:T(8,128)S(1)} %add.50), channel_id=1, source_target_pairs={{0,8},{2,10},{4,12},{6,14},{8,0},{10,2},{12,4},{14,6},{16,24},{18,... | collective-permute-start | bytes 3932168 | tf_op jit(solution)/shard_map/ppermute | solution.py:25
  391.9 58.3 %collective-permute-start.11 = (f32[512,640]{1,0:T(8,128)}, f32[512,640]{1,0:T(8,128)}, u32[]{:S(2)}, u32[]{:S(2)}) collective-permute-start(f32[512,640]{1,0:T(8,128)} %add.51), channel_id=1, source_target_pairs={{0,16},{2,18},{4,20},{6,22},{8,24},{10,26},{12,28},{14,30},{16,0},... | collective-permute-start | bytes 3932168 | tf_op jit(solution)/shard_map/ppermute | solution.py:25
